TPU v7x, 512 devices: a whole 4x4x16 slice. The times are simulated.
512 devices in a mesh: layer: 8 (over z_hi, x), row: 8 (over z_lo), col: 8 (over y, core).
Axes of the slice: x: 4, y: 4, z: 16 (z_hi: 2, z_lo: 8; z = z_hi * 8 + z_lo), core: 2. Of those that a mesh axis runs over, the one named last changes fastest.
Arguments:
- covariance: float32 [65536, 8192], P(('layer', 'row'), 'col'), parts along dimension 0, may hold values from -2 to 20, as said below
- weight: bfloat16 [65536, 2, 1024], P(('layer', 'col', 'row')), parts along dimension 0, may hold values from -6 to 6
- factor_a: bfloat16 [65536, 2, 256], P(('layer', 'col', 'row')), parts along dimension 0, may hold values from -1.5 to 1.5
- factor_b: bfloat16 [16, 256, 1024], P('layer', ('row', 'col')), parts along dimension 0, may hold values from -1.5 to 1.5
Outputs:
- new_a: float32 [65536, 2, 256], P(('layer', 'col', 'row')), parts along dimension 0
- new_b: float32 [16, 256, 1024], P('layer', ('row', 'col')), parts along dimension 0
There are 8 independent parts, one for each index of `layer`. A program takes and returns all parts, laid end to end along the dimension named above; each array names one. Nothing has to cross between parts.
Inputs may be any that keep to these rules, and one draw needn't show every extreme that they name: covariance is symmetric and positive definite.
All inputs are finite; a program needn't handle non-finite values.
Results may differ from a plain program's by a relative error of at most 0.0012.
Values may be sent and summed in bfloat16 or wider, within the bound.
A program may use at most 64 MiB of HBM per device.

v0:
```python
import jax
import jax.numpy as jnp
from jax import lax
from jax.sharding import PartitionSpec as P

D = 8192
O = 1024
R = 256


def reorder_slots(spread):
    side = lax.axis_size("row")
    total = side * side
    return spread.reshape(side, side, -1).transpose(1, 0, 2).reshape(total, -1)


def transpose_full(values):
    side = lax.axis_size("row")
    flat = values.reshape(side * side, -1)
    spread = lax.all_to_all(flat, ("row", "col"), split_axis=0, concat_axis=0, tiled=True)
    landed = lax.all_to_all(
        reorder_slots(spread), ("row", "col"), split_axis=0, concat_axis=0, tiled=True
    )
    return landed.reshape(values.shape)


def per_device(covariance, weight, factor_a, factor_b):
    highest = lax.Precision.HIGHEST
    row_count = weight.shape[0]
    full_b = lax.all_gather(factor_b, ("row", "col"), axis=1, tiled=True)
    right_f = full_b.astype(jnp.float32)
    diff_one = (
        weight.astype(jnp.float32)
        - jnp.einsum("nkr,kro->nko", factor_a, full_b, preferred_element_type=jnp.float32)
    ).astype(jnp.bfloat16)
    panels = jnp.einsum(
        "nko,kro->nkr",
        lax.all_gather(diff_one, "row", axis=0, tiled=True),
        full_b,
        preferred_element_type=jnp.float32,
    )
    panel_flat = panels.reshape(panels.shape[0], -1)
    cov_rows = covariance
    grad_one = lax.psum_scatter(
        jnp.dot(cov_rows, panel_flat, precision=highest, preferred_element_type=jnp.float32),
        "col",
        scatter_dimension=0,
        tiled=True,
    )
    grad_one = transpose_full(grad_one)
    new_a = factor_a.astype(jnp.float32) + 4.0 / O * grad_one.reshape(row_count, 2, R)
    diff_two = (
        weight.astype(jnp.float32) - jnp.einsum("nkr,kro->nko", new_a, right_f, precision=highest)
    ).astype(jnp.bfloat16)
    a_panel = lax.all_gather(new_a.reshape(row_count, 2 * R), "row", axis=0, tiled=True)
    cov_rows = covariance
    field = lax.psum_scatter(
        jnp.dot(cov_rows, a_panel, precision=highest, preferred_element_type=jnp.float32),
        "col",
        scatter_dimension=0,
        tiled=True,
    )
    field = transpose_full(field)
    partial_value = jnp.einsum(
        "nkr,nko->kro",
        field.reshape(row_count, 2, R),
        diff_two.astype(jnp.float32),
        precision=highest,
    )
    summed = lax.psum(partial_value, ("row", "col"))
    share_rows = factor_b.shape[1]
    linear_id = lax.axis_index("row") * lax.axis_size("col") + lax.axis_index("col")
    own_share = lax.dynamic_slice_in_dim(summed, linear_id * share_rows, share_rows, 1)
    new_b = factor_b.astype(jnp.float32) + 8.0 / D * own_share
    return (new_a, new_b)


def solution(mesh):
    in_specs = (
        P(("layer", "row"), "col"),
        P(("layer", "col", "row"), None, None),
        P(("layer", "col", "row"), None, None),
        P("layer", ("row", "col"), None),
    )
    out_specs = (P(("layer", "col", "row"), None, None), P("layer", ("row", "col"), None))
    return jax.shard_map(
        per_device, mesh=mesh, in_specs=in_specs, out_specs=out_specs, check_vma=False
    )
```

profile of v0, /device:TPU:1, one launch (start us, length us, event | category | flops | bytes accessed | tf_op | source)
XLA Modules:
  0.0 1366.5 jit_solution(1264701732032202692)
XLA Ops:
  7.2 1.3 copy.42
  8.6 1.4 copy.41
  10.0 125.7 %all-gather.4.cloned.1.call-done = bf16[2,256,1024]{2,0,1:T(2,128)(2,1)} async-done(((bf16[2,4,1024]{2,0,1:T(2,128)(2,1)}), bf16[2,256,1024]{2,0,1:T(2,128)(2,1)}) %all-gather.4.cloned.1.call-update) | async-done | bytes 1048592 | tf_op jit(solution)/shard_map/all_gather | solution.py:30
  135.7 2.7 fusion.3
  138.5 101.9 %all-gather.6.cloned.1.call-done = bf16[1024,2,1024]{0,2,1:T(8,128)(2,1)} async-done(((bf16[128,2,1024]{0,2,1:T(8,128)(2,1)}), bf16[1024,2,1024]{0,2,1:T(8,128)(2,1)}) %all-gather.6.cloned.1.call-update) | async-done | bytes 4194320 | tf_op jit(solution)/shard_map/all_gather | solution.py:38
  240.4 3.6 fusion.5
  244.0 8.3 convolution_bitcast_fusion.1
  252.3 39.2 %reduce-scatter.3.cloned.1.call-done = f32[128,512]{0,1:T(8,128)} async-done(((f32[1024,512]{0,1:T(8,128)}), f32[128,512]{0,1:T(8,128)}) %reduce-scatter.3.cloned.1.call-update) | async-done | bytes 262160 | tf_op jit(solution)/shard_map/reduce_scatter | solution.py:44
  291.5 1.1 copy.47
  292.9 32.7 %all_to_all.38 = f32[64,1,1024]{2,1,0:T(1,128)S(1)} all-to-all(f32[64,1,1024]{2,1,0:T(1,128)S(1)} %all_to_all.32), channel_id=1, replica_groups=mesh['layer'=8,'row'=8,'col'=8] {'row','col'}, dimensions={0} | all-to-all | bytes 524288 | tf_op jit(solution)/shard_map/all_to_all | solution.py:20
  326.1 25.6 %all_to_all.39 = f32[64,1,1024]{2,1,0:T(1,128)S(1)} all-to-all(f32[64,1,1024]{2,1,0:T(1,128)S(1)} %copy.50), channel_id=1, replica_groups=mesh['layer'=8,'row'=8,'col'=8] {'row','col'}, dimensions={0} | all-to-all | bytes 524288 | tf_op jit(solution)/shard_map/all_to_all | solution.py:21
  352.7 0.8 copy.65
  353.6 58.1 %all-gather.8.cloned.1.call-done = f32[1024,512]{1,0:T(8,128)} async-done(((f32[128,512]{1,0:T(8,128)}), f32[1024,512]{1,0:T(8,128)}) %all-gather.8.cloned.1.call-update) | async-done | bytes 2097168 | tf_op jit(solution)/shard_map/all_gather | solution.py:55
  411.7 16.7 %convolution_bitcast_fusion = f32[1024,512]{0,1:T(8,128)} fusion(f32[1024,512]{1,0:T(8,128)} %all-gather.8.cloned.1.call-done, f32[1024,1024]{1,0:T(8,128)} %param.4), kind=kOutput, calls=%fused_computation | convolution fusion | flops 6442450944 | bytes 8388608 | tf_op jit(solution)/shard_map/dot_general | solution.py:58
  428.4 40.4 %reduce-scatter.5.cloned.1.call-done = f32[128,512]{0,1:T(8,128)} async-done(((f32[1024,512]{0,1:T(8,128)}), f32[128,512]{0,1:T(8,128)}) %reduce-scatter.5.cloned.1.call-update) | async-done | bytes 262160 | tf_op jit(solution)/shard_map/reduce_scatter | solution.py:57
  468.8 1.1 copy.51
  470.2 32.8 %all_to_all.40 = f32[64,1,1024]{2,1,0:T(1,128)S(1)} all-to-all(f32[64,1,1024]{2,1,0:T(1,128)S(1)} %all_to_all.33), channel_id=1, replica_groups=mesh['layer'=8,'row'=8,'col'=8] {'row','col'}, dimensions={0} | all-to-all | bytes 524288 | tf_op jit(solution)/shard_map/all_to_all | solution.py:20
  503.2 1.0 copy.54
  504.2 5.9 all-to-all-start.3
  510.4 1.3 fusion.2
  511.8 18.2 %all-to-all-done.3 = f32[64,1,1024]{2,1,0:T(1,128)S(1)} async-done(((f32[64,1,1024]{2,1,0:T(1,128)}), f32[64,1,1024]{2,1,0:T(1,128)S(1)}, u32[]{:S(2)}, u32[]{:S(2)}) %all-to-all-start.3) | async-done | bytes 262176 | tf_op jit(solution)/shard_map/all_to_all | solution.py:21
  530.9 2.4 fusion.8
  533.2 825.0 %all-reduce.2.cloned.1.call-done = f32[2,256,1024]{2,1,0:T(8,128)} async-done(((f32[2,256,1024]{2,1,0:T(8,128)}), f32[2,256,1024]{2,1,0:T(8,128)}) %all-reduce.2.cloned.1.call-update) | async-done | bytes 2097168 | tf_op jit(solution)/shard_map/psum | solution.py:70
  1358.2 1.5 multiply_add_fusion
  (34 shorter events, 3.7 us)
Async XLA Ops:
  7.2 128.5 %all-gather.4.cloned.1.call-start = ((), (), s32[]{:S(2)}) async-start(), calls=%async_computation.6 | async-start | bytes 1064960 | tf_op jit(solution)/shard_map/all_gather | solution.py:30
  8.6 231.8 %all-gather.6.cloned.1.call-start = ((), (), s32[]{:S(2)}) async-start(), calls=%async_computation.7 | async-start | bytes 4718592 | tf_op jit(solution)/shard_map/all_gather | solution.py:38
  135.7 104.7 %copy-start.1 = (bf16[2,256,1024]{2,0,1:T(2,128)(2,1)S(1)}, bf16[2,256,1024]{2,0,1:T(2,128)(2,1)}, u32[]{:S(2)}) copy-start(bf16[2,256,1024]{2,0,1:T(2,128)(2,1)} %all-gather.4.cloned.1.call-done) | copy-start | bytes 3145732
  138.4 153.1 %reduce-scatter.3.cloned.1.call-start = ((), (), s32[]{:S(2)}) async-start(), calls=%async_computation.8 | async-start | bytes 2359296 | tf_op jit(solution)/shard_map/reduce_scatter | solution.py:44
  240.4 3.6 copy-start
  252.3 159.4 %all-gather.8.cloned.1.call-start = ((), (), s32[]{:S(2)}) async-start(), calls=%async_computation.9 | async-start | bytes 2359296 | tf_op jit(solution)/shard_map/all_gather | solution.py:55
  292.6 60.1 %copy-start.3 = (bf16[128,2,256]{2,1,0:T(2,128)(2,1)S(1)}, bf16[128,2,256]{2,1,0:T(2,128)(2,1)}, u32[]{:S(2)}) copy-start(bf16[128,2,256]{2,1,0:T(2,128)(2,1)} %param.6) | copy-start | bytes 393220
  352.7 157.7 %copy-start.2 = (f32[32,8,256]{2,1,0:T(8,128)}, f32[32,8,256]{2,1,0:T(8,128)S(1)}, u32[]{:S(2)}) copy-start(f32[32,8,256]{2,1,0:T(8,128)S(1)} %convert_add_fusion) | copy-start | bytes 786436
  353.5 115.2 %reduce-scatter.5.cloned.1.call-start = ((), (), s32[]{:S(2)}) async-start(), calls=%async_computation.10 | async-start | bytes 2359296 | tf_op jit(solution)/shard_map/reduce_scatter | solution.py:57
  504.2 25.8 %all-to-all-start.3 = ((f32[64,1,1024]{2,1,0:T(1,128)}), f32[64,1,1024]{2,1,0:T(1,128)S(1)}, u32[]{:S(2)}, u32[]{:S(2)}) async-start(f32[64,1,1024]{2,1,0:T(1,128)} %copy.54), calls=%async_computation.5 | async-start | bytes 524288 | tf_op jit(solution)/shard_map/all_to_all | solution.py:21
  510.2 848.1 %all-reduce.2.cloned.1.call-start = ((), (), s32[]{:S(2)}) async-start(), calls=%async_computation.11 | async-start | bytes 4194304 | tf_op jit(solution)/shard_map/psum | solution.py:70
  530.8 827.4 %copy-start.4 = (bf16[2,4,1024]{2,1,0:T(4,128)(2,1)S(1)}, bf16[2,4,1024]{2,1,0:T(4,128)(2,1)}, u32[]{:S(2)}) copy-start(bf16[2,4,1024]{2,1,0:T(4,128)(2,1)} %param.7) | copy-start | bytes 49156
Sparse Core Ops, SparseCore 0:
  10.7 124.9 all-gather.3
  138.6 101.7 all-gather.5
  252.4 39.0 reduce-scatter.2
  353.7 58.0 all-gather.7
  428.5 40.2 reduce-scatter.4
  533.4 824.8 all-reduce.1
where the time goes:
time: 1370 us
  waiting for transfers between devices  1210 us (88%)
  blocking collectives  91.1 us (7%)
  matrix products  34.9 us (3%)
  between operations  14.3 us (1%)
    psum x1, waiting for transfers between devices, per_device(): summed = lax.psum(partial_value, ('row', 'col'))  825 us
    all_gather x1, waiting for transfers between devices, per_device(): full_b = lax.all_gather(factor_b, ('row', 'col'), axis=1, tiled=True)  126 us
    all_gather x1, waiting for transfers between devices, per_device(): lax.all_gather(diff_one, 'row', axis=0, tiled=True)  102 us
    all_to_all x2, blocking collectives, transpose_full(): lax.all_to_all(flat, ('row', 'col'), split_axis=0, concat_axis=0, tiled=T...  65.6 us
    all_gather x1, waiting for transfers between devices, per_device(): lax.all_gather(new_a.reshape(row_count, 2 * R), 'row', axis=0, tiled=True)  58.1 us
    reduce_scatter x1, waiting for transfers between devices, per_device(): lax.psum_scatter(jnp.dot(cov_rows, a_panel, precision=highest, preferred_...  40.4 us
    reduce_scatter x1, waiting for transfers between devices, per_device(): lax.psum_scatter(jnp.dot(cov_rows, panel_flat, precision=highest, preferr...  39.2 us
  transfers between devices with their start and end apart: 7, of which 7 were waited for; matrix products, arithmetic and copies ran while one was open for 0% of the time, Pallas kernels for 0%

commit v1 on v0

--- a/solution.py
+++ b/solution.py
@@ -67,7 +67,7 @@
         diff_two.astype(jnp.float32),
         precision=highest,
     )
-    summed = lax.psum(partial_value, ("row", "col"))
+    summed = lax.psum(lax.psum(partial_value, "col"), "row")
     share_rows = factor_b.shape[1]
     linear_id = lax.axis_index("row") * lax.axis_size("col") + lax.axis_index("col")
     own_share = lax.dynamic_slice_in_dim(summed, linear_id * share_rows, share_rows, 1)

time: 1370 us -> 758 us (0.55)
  waiting for transfers between devices: 1210 us -> 595 us
    psum x1 -> x2, waiting for transfers between devices: 825 us -> 212 us  [per_device(): summed = lax.psum(lax.psum(partial_value, 'col'), 'row')]
  transfers between devices with their start and end apart: 7 -> 8, of which waited for: 7 -> 8; matrix products, arithmetic and copies ran while one was open for 0% -> 0% of each run, Pallas kernels for 0% -> 0%
where the time goes in v1:
time: 758 us; the launch traced here: 753 us
  waiting for transfers between devices  595 us (78%)
  blocking collectives  91.1 us (12%)
  matrix products  34.9 us (5%)
  between operations  14.3 us (2%)
  local copies, waits for them, and re-layouts  8.4 us (1%)
    psum x2, waiting for transfers between devices, per_device(): summed = lax.psum(lax.psum(partial_value, 'col'), 'row')  212 us
    all_gather x1, waiting for transfers between devices, per_device(): full_b = lax.all_gather(factor_b, ('row', 'col'), axis=1, tiled=True)  126 us
    all_gather x1, waiting for transfers between devices, per_device(): lax.all_gather(diff_one, 'row', axis=0, tiled=True)  102 us
    all_to_all x2, blocking collectives, transpose_full(): lax.all_to_all(flat, ('row', 'col'), split_axis=0, concat_axis=0, tiled=T...  65.6 us
    all_gather x1, waiting for transfers between devices, per_device(): lax.all_gather(new_a.reshape(row_count, 2 * R), 'row', axis=0, tiled=True)  58.1 us
    reduce_scatter x1, waiting for transfers between devices, per_device(): lax.psum_scatter(jnp.dot(cov_rows, a_panel, precision=highest, preferred_...  40.4 us
    reduce_scatter x1, waiting for transfers between devices, per_device(): lax.psum_scatter(jnp.dot(cov_rows, panel_flat, precision=highest, preferr...  39.2 us
    all_to_all x1, blocking collectives, transpose_full(): lax.all_to_all(reorder_slots(spread), ('row', 'col'), split_axis=0, conca...  25.6 us
  transfers between devices with their start and end apart: 8, of which 8 were waited for; matrix products, arithmetic and copies ran while one was open for 0% of the time, Pallas kernels for 0%

profile of v1, /device:TPU:1, one launch (start us, length us, event | category | flops | bytes accessed | tf_op | source)
XLA Modules:
  0.0 753.4 jit_solution(11887402358408191390)
XLA Ops:
  7.2 1.3 copy.42
  8.6 1.4 copy.41
  10.0 125.7 %all-gather.4.cloned.1.call-done = bf16[2,256,1024]{2,0,1:T(2,128)(2,1)} async-done(((bf16[2,4,1024]{2,0,1:T(2,128)(2,1)}), bf16[2,256,1024]{2,0,1:T(2,128)(2,1)}) %all-gather.4.cloned.1.call-update) | async-done | bytes 1048592 | tf_op jit(solution)/shard_map/all_gather | solution.py:30
  135.7 2.7 fusion.3
  138.5 101.9 %all-gather.6.cloned.1.call-done = bf16[1024,2,1024]{0,2,1:T(8,128)(2,1)} async-done(((bf16[128,2,1024]{0,2,1:T(8,128)(2,1)}), bf16[1024,2,1024]{0,2,1:T(8,128)(2,1)}) %all-gather.6.cloned.1.call-update) | async-done | bytes 4194320 | tf_op jit(solution)/shard_map/all_gather | solution.py:38
  240.4 3.6 fusion.5
  244.0 8.3 %convolution_bitcast_fusion.1 = f32[1024,512]{0,1:T(8,128)} fusion(f32[1024,512]{0,1:T(8,128)S(1)} %bitcast.46, f32[1024,1024]{1,0:T(8,128)S(1)} %copy-done), kind=kOutput, calls=%fused_computation.1 | convolution fusion | flops 6442450944 | bytes 8388608 | tf_op jit(solution)/shard_map/dot_general | solution.py:45
  252.3 39.2 %reduce-scatter.3.cloned.1.call-done = f32[128,512]{0,1:T(8,128)} async-done(((f32[1024,512]{0,1:T(8,128)}), f32[128,512]{0,1:T(8,128)}) %reduce-scatter.3.cloned.1.call-update) | async-done | bytes 262160 | tf_op jit(solution)/shard_map/reduce_scatter | solution.py:44
  291.5 1.1 copy.47
  292.9 32.7 %all_to_all.38 = f32[64,1,1024]{2,1,0:T(1,128)S(1)} all-to-all(f32[64,1,1024]{2,1,0:T(1,128)S(1)} %all_to_all.32), channel_id=1, replica_groups=mesh['layer'=8,'row'=8,'col'=8] {'row','col'}, dimensions={0} | all-to-all | bytes 524288 | tf_op jit(solution)/shard_map/all_to_all | solution.py:20
  326.1 25.6 %all_to_all.39 = f32[64,1,1024]{2,1,0:T(1,128)S(1)} all-to-all(f32[64,1,1024]{2,1,0:T(1,128)S(1)} %copy.50), channel_id=1, replica_groups=mesh['layer'=8,'row'=8,'col'=8] {'row','col'}, dimensions={0} | all-to-all | bytes 524288 | tf_op jit(solution)/shard_map/all_to_all | solution.py:21
  353.6 58.1 %all-gather.8.cloned.1.call-done = f32[1024,512]{1,0:T(8,128)} async-done(((f32[128,512]{1,0:T(8,128)}), f32[1024,512]{1,0:T(8,128)}) %all-gather.8.cloned.1.call-update) | async-done | bytes 2097168 | tf_op jit(solution)/shard_map/all_gather | solution.py:55
  411.7 16.7 %convolution_bitcast_fusion = f32[1024,512]{0,1:T(8,128)} fusion(f32[1024,512]{1,0:T(8,128)} %all-gather.8.cloned.1.call-done, f32[1024,1024]{1,0:T(8,128)} %param.4), kind=kOutput, calls=%fused_computation | convolution fusion | flops 6442450944 | bytes 8388608 | tf_op jit(solution)/shard_map/dot_general | solution.py:58
  428.4 40.4 %reduce-scatter.5.cloned.1.call-done = f32[128,512]{0,1:T(8,128)} async-done(((f32[1024,512]{0,1:T(8,128)}), f32[128,512]{0,1:T(8,128)}) %reduce-scatter.5.cloned.1.call-update) | async-done | bytes 262160 | tf_op jit(solution)/shard_map/reduce_scatter | solution.py:57
  468.8 1.1 copy.51
  470.2 32.8 %all_to_all.40 = f32[64,1,1024]{2,1,0:T(1,128)S(1)} all-to-all(f32[64,1,1024]{2,1,0:T(1,128)S(1)} %all_to_all.33), channel_id=1, replica_groups=mesh['layer'=8,'row'=8,'col'=8] {'row','col'}, dimensions={0} | all-to-all | bytes 524288 | tf_op jit(solution)/shard_map/all_to_all | solution.py:20
  503.2 1.0 copy.54
  504.2 5.9 all-to-all-start.3
  510.4 1.3 fusion.2
  511.8 18.2 %all-to-all-done.3 = f32[64,1,1024]{2,1,0:T(1,128)S(1)} async-done(((f32[64,1,1024]{2,1,0:T(1,128)}), f32[64,1,1024]{2,1,0:T(1,128)S(1)}, u32[]{:S(2)}, u32[]{:S(2)}) %all-to-all-start.3) | async-done | bytes 262176 | tf_op jit(solution)/shard_map/all_to_all | solution.py:21
  530.8 2.3 fusion.8
  533.3 71.6 %all-reduce.3.cloned.1.call-done = f32[2,256,1024]{2,1,0:T(8,128)} async-done(((f32[2,256,1024]{2,1,0:T(8,128)}), f32[2,256,1024]{2,1,0:T(8,128)}) %all-reduce.3.cloned.1.call-update) | async-done | bytes 2097168 | tf_op jit(solution)/shard_map/psum | solution.py:70
  604.9 140.2 %all-reduce.5.cloned.1.call-done = f32[2,256,1024]{2,1,0:T(8,128)} async-done(((f32[2,256,1024]{2,1,0:T(8,128)}), f32[2,256,1024]{2,1,0:T(8,128)}) %all-reduce.5.cloned.1.call-update) | async-done | bytes 2097168 | tf_op jit(solution)/shard_map/psum | solution.py:70
  745.1 1.5 multiply_add_fusion
  (37 shorter events, 4.5 us)
Async XLA Ops:
  7.2 128.5 %all-gather.4.cloned.1.call-start = ((), (), s32[]{:S(2)}) async-start(), calls=%async_computation.6 | async-start | bytes 1064960 | tf_op jit(solution)/shard_map/all_gather | solution.py:30
  8.6 231.8 %all-gather.6.cloned.1.call-start = ((), (), s32[]{:S(2)}) async-start(), calls=%async_computation.7 | async-start | bytes 4718592 | tf_op jit(solution)/shard_map/all_gather | solution.py:38
  135.7 104.7 %copy-start.1 = (bf16[2,256,1024]{2,0,1:T(2,128)(2,1)S(1)}, bf16[2,256,1024]{2,0,1:T(2,128)(2,1)}, u32[]{:S(2)}) copy-start(bf16[2,256,1024]{2,0,1:T(2,128)(2,1)} %all-gather.4.cloned.1.call-done) | copy-start | bytes 3145732
  138.4 153.1 %reduce-scatter.3.cloned.1.call-start = ((), (), s32[]{:S(2)}) async-start(), calls=%async_computation.8 | async-start | bytes 2359296 | tf_op jit(solution)/shard_map/reduce_scatter | solution.py:44
  240.4 3.6 copy-start
  252.3 159.4 %all-gather.8.cloned.1.call-start = ((), (), s32[]{:S(2)}) async-start(), calls=%async_computation.9 | async-start | bytes 2359296 | tf_op jit(solution)/shard_map/all_gather | solution.py:55
  292.6 60.1 %copy-start.3 = (bf16[128,2,256]{2,1,0:T(2,128)(2,1)S(1)}, bf16[128,2,256]{2,1,0:T(2,128)(2,1)}, u32[]{:S(2)}) copy-start(bf16[128,2,256]{2,1,0:T(2,128)(2,1)} %param.6) | copy-start | bytes 393220
  352.7 157.7 %copy-start.2 = (f32[32,8,256]{2,1,0:T(8,128)}, f32[32,8,256]{2,1,0:T(8,128)S(1)}, u32[]{:S(2)}) copy-start(f32[32,8,256]{2,1,0:T(8,128)S(1)} %convert_add_fusion) | copy-start | bytes 786436
  353.5 115.2 %reduce-scatter.5.cloned.1.call-start = ((), (), s32[]{:S(2)}) async-start(), calls=%async_computation.10 | async-start | bytes 2359296 | tf_op jit(solution)/shard_map/reduce_scatter | solution.py:57
  504.2 25.8 %all-to-all-start.3 = ((f32[64,1,1024]{2,1,0:T(1,128)}), f32[64,1,1024]{2,1,0:T(1,128)S(1)}, u32[]{:S(2)}, u32[]{:S(2)}) async-start(f32[64,1,1024]{2,1,0:T(1,128)} %copy.54), calls=%async_computation.5 | async-start | bytes 524288 | tf_op jit(solution)/shard_map/all_to_all | solution.py:21
  510.2 94.7 %all-reduce.3.cloned.1.call-start = ((), (), s32[]{:S(2)}) async-start(), calls=%async_computation.11 | async-start | bytes 4194304 | tf_op jit(solution)/shard_map/psum | solution.py:70
  533.2 211.9 %copy-start.4 = (bf16[2,4,1024]{2,1,0:T(4,128)(2,1)S(1)}, bf16[2,4,1024]{2,1,0:T(4,128)(2,1)}, u32[]{:S(2)}) copy-start(bf16[2,4,1024]{2,1,0:T(4,128)(2,1)} %param.7) | copy-start | bytes 49156
  533.2 211.8 %all-reduce.5.cloned.1.call-start = ((), (), s32[]{:S(2)}) async-start(), calls=%async_computation.12 | async-start | bytes 4194304 | tf_op jit(solution)/shard_map/psum | solution.py:70
Sparse Core Ops, SparseCore 0:
  10.7 124.9 all-gather.3
  138.6 101.7 all-gather.5
  252.4 39.0 reduce-scatter.2
  353.7 58.0 all-gather.7
  428.5 40.2 reduce-scatter.4
  533.3 71.4 all-reduce.2
  607.8 137.1 all-reduce.4
